TPU v7x, 128 devices: a whole 4x4x4 slice. The times are simulated.
128 devices in a mesh: pipe: 4 (over y_hi, core), dp: 32 (over x, y_lo, z).
Axes of the slice: x: 4, y: 4 (y_hi: 2, y_lo: 2; y = y_hi * 2 + y_lo), z: 4, core: 2. Of those that a mesh axis runs over, the one named last changes fastest.
Arguments:
- enc_out: bfloat16 [4, 4096, 2048], P('pipe', 'dp'), may hold values from -6 to 6
- kv_weight: bfloat16 [4, 2048, 4096], P('pipe'), may hold values from -0.125 to 0.125
- queries: bfloat16 [4, 4, 1024, 2048], P('pipe', None, 'dp'), may hold values from -0.375 to 0.375
- out_grad: bfloat16 [4, 4, 1024, 2048], P('pipe', None, 'dp'), may hold values from -24 to 24
Outputs:
- grad_kv: float32 [4, 2048, 4096], P('pipe', 'dp')
- grad_enc: float32 [4, 4096, 2048], P('pipe', 'dp')
- grad_query: bfloat16 [4, 4, 1024, 2048], P('pipe', None, 'dp')
All inputs are finite; a program needn't handle non-finite values.
Results may differ from a plain program's by a relative error of at most 0.013.
Values may be sent and summed in bfloat16 or wider, within the bound.
A program may use at most 192 MiB of HBM per device.

v0:
```python
import jax
import jax.numpy as jnp
from jax import lax
from jax.sharding import PartitionSpec as P

HEADS = 8
HD = 256
INNER = 2048


def per_device(enc_out, kv_weight, queries, out_grad):
    gathered = lax.all_gather(enc_out, "pipe", axis=0, tiled=True)
    micro = gathered.shape[0]
    length = gathered.shape[1]
    dec_len = queries.shape[2]
    weight = kv_weight[0]
    key_value = jnp.einsum(
        "mtd,dc->mtc", gathered, weight, preferred_element_type=jnp.float32
    ).astype(jnp.bfloat16)
    key_heads = key_value[..., :INNER].reshape(micro, length, HEADS, HD)
    value_heads = key_value[..., INNER:].reshape(micro, length, HEADS, HD)
    query_heads = queries[0].reshape(micro, dec_len, HEADS, HD)
    grad_heads = out_grad[0].reshape(micro, dec_len, HEADS, HD)
    raw_scores = jnp.einsum(
        "mqhd,mkhd->mhqk", query_heads, key_heads, preferred_element_type=jnp.float32
    )
    attn_probs = jax.nn.softmax(raw_scores, axis=-1)
    probs_low = attn_probs.astype(jnp.bfloat16)
    prob_grad = jnp.einsum(
        "mqhd,mkhd->mhqk", grad_heads, value_heads, preferred_element_type=jnp.float32
    )
    row_total = jnp.sum(attn_probs * prob_grad, axis=-1, keepdims=True)
    score_low = (attn_probs * (prob_grad - row_total)).astype(jnp.bfloat16)
    query_grad = jnp.einsum(
        "mhqk,mkhd->mqhd", score_low, key_heads, preferred_element_type=jnp.float32
    ).astype(jnp.bfloat16)
    key_grad = jnp.einsum(
        "mhqk,mqhd->mkhd", score_low, query_heads, preferred_element_type=jnp.float32
    ).astype(jnp.bfloat16)
    value_grad = jnp.einsum(
        "mhqk,mqhd->mkhd", probs_low, grad_heads, preferred_element_type=jnp.float32
    ).astype(jnp.bfloat16)
    kv_grad = jnp.concatenate(
        [key_grad.reshape(micro, length, INNER), value_grad.reshape(micro, length, INNER)], axis=-1
    )
    weight_term = jnp.einsum("mtd,mtc->dc", gathered, kv_grad, preferred_element_type=jnp.float32)
    weight_sum = lax.psum_scatter(weight_term, "dp", scatter_dimension=0, tiled=True)
    enc_term = jnp.einsum("mtc,dc->mtd", kv_grad, weight, preferred_element_type=jnp.float32)
    enc_sum = lax.psum_scatter(enc_term, "pipe", scatter_dimension=0, tiled=True)
    return (weight_sum[None], enc_sum, query_grad.reshape(1, micro, dec_len, INNER))


def solution(mesh):
    placed = (
        P("pipe", "dp", None),
        P("pipe", None, None),
        P("pipe", None, "dp", None),
        P("pipe", None, "dp", None),
    )
    return jax.shard_map(
        per_device,
        mesh=mesh,
        in_specs=placed,
        out_specs=(P("pipe", "dp", None), P("pipe", "dp", None), P("pipe", None, "dp", None)),
        check_vma=False,
    )
```

profile of v0, /device:TPU:0, one launch (start us, length us, event | category | flops | bytes accessed | tf_op | source)
XLA Modules:
  0.0 542.1 jit_solution(4809124018436357373)
XLA Ops:
  7.2 0.7 all-gather.2.cloned.1.call-update
  7.9 1.2 copy.45
  9.1 2.0 copy.46
  11.1 27.8 %all-gather.2.cloned.1.call-done = bf16[4,128,2048]{2,1,0:T(8,128)(2,1)} async-done(((bf16[1,128,2048]{2,1,0:T(8,128)(2,1)}), bf16[4,128,2048]{2,1,0:T(8,128)(2,1)}) %all-gather.2.cloned.1.call-update) | async-done | bytes 2097168 | tf_op jit(solution)/shard_map/all_gather | solution.py:12
  38.8 13.0 %fusion.5 = bf16[4,128,4096]{2,1,0:T(8,128)(2,1)S(1)} fusion(bf16[4,128,2048]{2,1,0:T(8,128)(2,1)} %all-gather.2.cloned.1.call-done, bf16[1,2048,4096]{2,1,0:T(8,128)(2,1)} %param.5), kind=kOutput, calls=%fused_computation.6 | convolution fusion | flops 8592031744 | bytes 23068672 | tf_op jit(solution)/shard_map/mtd,dc->mtc/dot_general | solution.py:17
  51.8 1.8 fusion.38
  53.7 0.8 fusion.25
  54.5 5.4 %fusion.39 = (f32[4,8,32]{2,1,0:T(8,128)S(1)}, f32[4,8,32,128]{3,2,1,0:T(8,128)S(1)}) fusion(f32[4,8,32,128]{3,2,1,0:T(8,128)S(1)} %fusion.25), kind=kOutput, calls=%fused_computation.36 | output fusion | flops 262271 | bytes 1052672 | tf_op jit(solution)/shard_map/sub | solution.py:27
  59.9 3.9 convert_bitcast_fusion
  63.8 2.4 copy.35
  66.2 2.6 multiply_reduce_fusion
  69.1 0.8 convert_bitcast_fusion.1
  69.9 2.4 copy.33
  72.3 16.6 %convolution_bitcast_fusion = f32[2048,4096]{0,1:T(8,128)} fusion(bf16[4,128,2048]{2,1,0:T(8,128)(2,1)} %all-gather.2.cloned.1.call-done, bf16[4,128,2048]{1,2,0:T(8,128)(2,1)} %bitcast.67, bf16[4,128,2048]{1,2,0:T(8,128)(2,1)} %bitcast.69), kind=kOutput, calls=%fused_computation.1 | convolution fusion | flops 8598323200 | bytes 39845888 | tf_op jit(solution)/shard_map/mtd,mtc->dc/dot_general | solution.py:46
  89.0 31.1 %copy.41 = f32[2048,4096]{1,0:T(8,128)} copy(f32[2048,4096]{0,1:T(8,128)} %convolution_bitcast_fusion) | data formatting | bytes 67108864
  120.3 1.3 copy-done.2
  121.6 14.5 %fusion.1 = f32[4,128,2048]{2,1,0:T(8,128)} fusion(bf16[1,2048,4096]{2,1,0:T(8,128)(2,1)} %param.5, bf16[4,128,2048]{1,2,0:T(8,128)(2,1)S(1)} %bitcast.68, bf16[4,128,2048]{1,2,0:T(8,128)(2,1)} %bitcast.70), kind=kOutput, calls=%fused_computation.2 | convolution fusion | flops 8598323200 | bytes 25165824 | tf_op jit(solution)/shard_map/mtc,dc->mtd/dot_general | solution.py:48
  136.2 1.6 copy-done.1
  137.7 0.4 fusion.22
  138.4 1.0 reshape.28
  139.5 344.8 %reduce-scatter.7.cloned.1.call-done = f32[64,4096]{1,0:T(8,128)} async-done(((f32[2048,4096]{1,0:T(8,128)}), f32[64,4096]{1,0:T(8,128)}) %reduce-scatter.7.cloned.1.call-update) | async-done | bytes 1048592
  484.3 1.8 copy.42
  486.1 1.6 copy.39
  487.7 47.8 %reduce-scatter.5.cloned.1.call-done = f32[1,128,2048]{2,1,0:T(8,128)} async-done(((f32[4,128,2048]{2,1,0:T(8,128)}), f32[1,128,2048]{2,1,0:T(8,128)}) %reduce-scatter.5.cloned.1.call-update) | async-done | bytes 1048592 | tf_op jit(solution)/shard_map/reduce_scatter | solution.py:49
  (13 shorter events, 1.0 us)
Async XLA Ops:
  7.2 31.6 %all-gather.2.cloned.1.call-start = ((), (), s32[]{:S(2)}) async-start(), calls=%async_computation.2 | async-start | bytes 2621440 | tf_op jit(solution)/shard_map/all_gather | solution.py:12
  7.9 476.4 %reduce-scatter.7.cloned.1.call-start = ((), (), s32[]{:S(2)}) async-start(), calls=%async_computation.4 | async-start | bytes 34603008
  53.7 6.3 %copy-start = (bf16[4,128,2048]{2,1,0:T(8,128)(2,1)}, bf16[4,128,2048]{2,1,0:T(8,128)(2,1)S(1)}, u32[]{:S(2)}) copy-start(bf16[4,128,2048]{2,1,0:T(8,128)(2,1)S(1)} %get-tuple-element.13) | copy-start | bytes 6291460
  54.5 5.4 %copy-start.3 = (f32[4,8,32,128]{3,2,1,0:T(8,128)}, f32[4,8,32,128]{3,2,1,0:T(8,128)S(1)}, u32[]{:S(2)}) copy-start(f32[4,8,32,128]{3,2,1,0:T(8,128)S(1)} %fusion.25) | copy-start | bytes 1572868
  120.1 1.6 copy-start.2
  120.1 415.4 %reduce-scatter.5.cloned.1.call-start = ((), (), s32[]{:S(2)}) async-start(), calls=%async_computation.3 | async-start | bytes 5242880 | tf_op jit(solution)/shard_map/reduce_scatter | solution.py:49
  136.1 1.6 copy-start.1
Sparse Core Ops, SparseCore 0:
  9.7 29.0 all-gather.1
  120.2 364.0 reduce-scatter.6
  487.5 47.9 reduce-scatter.4
where the time goes:
time: 544 us; the launch traced here: 542 us
  waiting for transfers between devices  421 us (77%)
  matrix products  52.5 us (10%)
  local copies, waits for them, and re-layouts  48.5 us (9%)
  between operations  13.8 us (3%)
  other arithmetic  5.77 us (1%)
    unnamed x4, waiting for transfers between devices  346 us
    reduce_scatter x1, waiting for transfers between devices, per_device(): lax.psum_scatter(enc_term, 'pipe', scatter_dimension=0, tiled=True)  47.8 us
    unnamed x13, local copies, waits for them, and re-layouts  40.5 us
    all_gather x1, waiting for transfers between devices, per_device(): gathered = lax.all_gather(enc_out, 'pipe', axis=0, tiled=True)  27.8 us
    dot_general x1, matrix products, per_device(): jnp.einsum('mtd,mtc->dc', gathered, kv_grad, preferred_element_type=jnp.f...  16.6 us
    dot_general x1, matrix products, per_device(): jnp.einsum('mtc,dc->mtd', kv_grad, weight, preferred_element_type=jnp.flo...  14.5 us
    dot_general x1, matrix products, per_device(): jnp.einsum('mtd,dc->mtc', gathered, weight, preferred_element_type=jnp.fl...  13 us
  transfers between devices with their start and end apart: 3, of which 3 were waited for; matrix products, arithmetic and copies ran while one was open for 4% of the time, Pallas kernels for 0%

commit v1 on v0

v1 whole, which is shorter than its diff:
```python
import jax
import jax.numpy as jnp
from jax import lax
from jax.experimental import pallas as pl
from jax.experimental.pallas import tpu as pltpu
from jax.sharding import PartitionSpec as P

HD = 256
INNER = 2048
D = 2048
LEN = 128
Q = 32
BF = jnp.bfloat16
F32 = jnp.float32
MESH = pl.DeviceIdType.MESH

ENC, QG, SC, P1, P2, P3, E1, E2, NSEM = 0, 7, 15, 19, 43, 67, 75, 79, 83


def body(enc_hbm, w_hbm, q_hbm, g_hbm, gkv_hbm, genc_hbm, gq_hbm,
         w, encb, enct, kv, qb, gb, qgn, gqb, sco, sci, rhs, part, r1, r2, x3, r3, outb,
         ek, es, er, ys, yr, lsem, wsem, ssem, rsem):
    p = lax.axis_index("pipe")
    d = lax.axis_index("dp")
    yh, c = p // 2, p % 2
    x, yl, z = d // 8, (d // 4) % 2, d % 4
    po = 2 * yh + 1 - c
    pp = 2 * (1 - yh) + c
    ppo = 2 * (1 - yh) + 1 - c
    dn = x * 8 + (1 - yl) * 4 + z
    core, partner, near, far = (po, d), (pp, d), (p, dn), (pp, dn)

    def peer(half_axis, k):
        if half_axis == 0:
            return (p, lax.rem(x + k, 4) * 8 + yl * 4 + z)
        return (p, x * 8 + yl * 4 + lax.rem(z + k, 4))

    def rc(src, dst, idx, dev):
        return pltpu.make_async_remote_copy(
            src_ref=src, dst_ref=dst, send_sem=ssem.at[idx], recv_sem=rsem.at[idx],
            device_id=dev, device_id_type=MESH)

    def got(dst, idx):
        rc(dst, dst, idx, core).wait_recv()

    def w_copy(j):
        cols = pl.ds(pl.multiple_of(j * 256, 256), 256)
        return pltpu.make_async_copy(w_hbm.at[0, :, cols], w.at[:, cols], wsem.at[j])

    own_enc = pltpu.make_async_copy(enc_hbm.at[0], encb.at[p], lsem.at[0])
    own_q = pltpu.make_async_copy(q_hbm.at[0], qb, lsem.at[1])
    own_g = pltpu.make_async_copy(g_hbm.at[0], gb, lsem.at[2])
    own_enc.start()

    @pl.loop(0, 16)
    def _(j):
        w_copy(j).start()

    own_q.start()
    own_g.start()

    barrier = pltpu.get_barrier_semaphore()
    others = [core, partner, near, far] + [peer(h, k) for h in (0, 1) for k in (1, 2, 3)]
    for dev in others:
        pl.semaphore_signal(barrier, inc=1, device_id=dev, device_id_type=MESH)
    pl.semaphore_wait(barrier, len(others))

    sends = []

    def send(src, dst, idx, dev):
        cp = rc(src, dst, idx, dev)
        cp.start()
        sends.append(cp)

    send(enc_hbm.at[0], encb.at[p], ENC + 0, core)
    send(enc_hbm.at[0], encb.at[p], ENC + 1, partner)

    def project(first, j):
        cols = pl.ds(pl.multiple_of(j * 256, 256), 256)
        rows = encb[pl.ds(first, 2)].reshape(256, D)
        out = jnp.dot(rows, w[:, cols], preferred_element_type=F32)
        kv[pl.ds(first, 2), :, cols] = out.astype(BF).reshape(2, LEN, 256)

    def transpose(slot):
        cols = pl.ds(pl.multiple_of(slot * LEN, LEN), LEN)

        @pl.loop(0, 8)
        def _(b):
            rows = pl.ds(pl.multiple_of(b * 256, 256), 256)
            enct[rows, cols] = encb[slot, :, rows].T

    own_enc.wait()
    got(encb.at[po], ENC + 0)

    @pl.loop(0, 16)
    def _(j):
        w_copy(j).wait()
        project(2 * yh, j)

    own_q.wait()
    own_g.wait()
    send(enc_hbm.at[0], encb.at[4 + p], ENC + 2, near)
    send(enc_hbm.at[0], encb.at[4 + p], ENC + 3, far)
    for i in range(4):
        cols = pl.ds(pl.multiple_of((1 - yl) * 1024 + i * 256, 256), 256)
        send(qb.at[:, :, cols], qgn.at[i, 0], QG + 2 * i, near)
        send(gb.at[:, :, cols], qgn.at[i, 1], QG + 2 * i + 1, near)
    transpose(p)
    transpose(po)
    got(encb.at[pp], ENC + 1)
    send(encb.at[pp], encb.at[pp], ENC + 4, core)
    transpose(pp)
    got(encb.at[ppo], ENC + 4)
    transpose(ppo)

    tl = (((0,), (0,)), ((), ()))
    nt = (((1,), (1,)), ((), ()))

    def attend(i, slot):
        @pl.loop(0, 4)
        def _(t):
            project(2 * (1 - yh), i + 4 * t)

        units = []
        for own in (0, 1):
            head = (yl if own else 1 - yl) * 4 + i
            kc = pl.ds(pl.multiple_of(head * HD, HD), HD)
            vc = pl.ds(pl.multiple_of(INNER + head * HD, HD), HD)
            for m in range(4):
                units.append((own, kc, vc, m))
        raws, pgs = [], []
        for own, kc, vc, m in units:
            raws.append(lax.dot_general(qb[m, :, kc], kv[m, :, kc], nt, preferred_element_type=F32))
            pgs.append(lax.dot_general(gb[m, :, kc], kv[m, :, vc], nt, preferred_element_type=F32))
        raw = jnp.concatenate(raws, axis=0)
        pg = jnp.concatenate(pgs, axis=0)
        e = jnp.exp(raw - jnp.max(raw, axis=-1, keepdims=True))
        prob = e / jnp.sum(e, axis=-1, keepdims=True)
        total = jnp.sum(prob * pg, axis=-1, keepdims=True)
        score = (prob * (pg - total)).astype(BF)
        low = prob.astype(BF)
        for n, (own, kc, vc, m) in enumerate(units):
            s_n, p_n = score[n * Q:(n + 1) * Q], low[n * Q:(n + 1) * Q]
            gqb[m, :, kc] = jnp.dot(s_n, kv[m, :, kc], preferred_element_type=F32).astype(BF)
            kg = lax.dot_general(s_n, qb[m, :, kc], tl, preferred_element_type=F32).astype(BF)
            vg = lax.dot_general(p_n, gb[m, :, kc], tl, preferred_element_type=F32).astype(BF)
            kv[m, :, kc] = kg
            kv[m, :, vc] = vg
            if own:
                rhs[slot, m * LEN:(m + 1) * LEN, 0:HD] = kg
                rhs[slot, m * LEN:(m + 1) * LEN, HD:2 * HD] = vg
            else:
                sco[i, 0, m] = s_n
                sco[i, 1, m] = p_n
        send(sco.at[i], sci.at[i], SC + i, near)

    def weight(i, slot):
        got(sci.at[i], SC + i)
        got(qgn.at[i, 0], QG + 2 * i)
        got(qgn.at[i, 1], QG + 2 * i + 1)
        for m in range(4):
            kg = lax.dot_general(sci[i, 0, m], qgn[i, 0, m], tl, preferred_element_type=F32)
            vg = lax.dot_general(sci[i, 1, m], qgn[i, 1, m], tl, preferred_element_type=F32)
            rhs[slot, 512 + m * LEN:512 + (m + 1) * LEN, 0:HD] = kg.astype(BF)
            rhs[slot, 512 + m * LEN:512 + (m + 1) * LEN, HD:2 * HD] = vg.astype(BF)

        @pl.loop(0, 4)
        def _(xp):
            rows = pl.ds(pl.multiple_of(xp * 512, 512), 512)
            for half in (0, 1):
                out = jnp.dot(enct[rows, :], rhs[slot, :, half * HD:(half + 1) * HD],
                              preferred_element_type=F32).astype(BF)
                for yy in range(2):
                    for zz in range(4):
                        piece = out[yy * 256 + zz * 64:yy * 256 + zz * 64 + 64]
                        if half == 0:
                            part[i, 0, xp, zz * 128 + yy * 64:zz * 128 + yy * 64 + 64] = piece
                        else:
                            at = pl.multiple_of(xp * 128 + yy * 64, 64)
                            part[i, 1, zz, pl.ds(at, 64)] = piece

    first = (x, z)
    second = (z, x)

    def send1(i):
        for half in (0, 1):
            for k in (1, 2, 3):
                send(part.at[i, half, lax.rem(first[half] + k, 4)], r1.at[i, half, k - 1],
                     P1 + (2 * i + half) * 3 + k - 1, peer(half, k))

    def reduce1(i):
        for half in (0, 1):
            a = first[half]
            for k in (1, 2, 3):
                got(r1.at[i, half, k - 1], P1 + (2 * i + half) * 3 + k - 1)

            @pl.loop(0, 8)
            def _(b):
                rows = pl.ds(pl.multiple_of(b * 64, 64), 64)
                acc = part[i, half, a, rows].astype(F32)
                for k in range(3):
                    acc += r1[i, half, k, rows].astype(F32)
                part[i, half, a, rows] = acc.astype(BF)

            for k in (1, 2, 3):
                rows = pl.ds(pl.multiple_of(lax.rem(second[half] + k, 4) * 128, 128), 128)
                send(part.at[i, half, a, rows], r2.at[i, half, k - 1],
                     P2 + (2 * i + half) * 3 + k - 1, peer(1 - half, k))

    def reduce2(i):
        for half in (0, 1):
            a = first[half]
            for k in (1, 2, 3):
                got(r2.at[i, half, k - 1], P2 + (2 * i + half) * 3 + k - 1)

            def total(which):
                at = pl.ds(pl.multiple_of(second[half] * 128 + which * 64, 64), 64)
                rows = pl.ds(pl.multiple_of(which * 64, 64), 64)
                acc = part[i, half, a, at].astype(F32)
                for k in range(3):
                    acc += r2[i, half, k, rows].astype(F32)
                return acc

            x3[i, half] = total(1 - yl).astype(BF)
            send(x3.at[i, half], r3.at[i, half], P3 + 2 * i + half, near)
            cols = pl.ds(pl.multiple_of(half * INNER + (yl * 4 + i) * HD, HD), HD)
            outb[:, cols] = total(yl)

    def finish(i):
        for half in (0, 1):
            got(r3.at[i, half], P3 + 2 * i + half)
            cols = pl.ds(pl.multiple_of(half * INNER + ((1 - yl) * 4 + i) * HD, HD), HD)
            outb[:, cols] = r3[i, half].astype(F32)

    def enc_term(piece):
        @pl.loop(0, 2)
        def _(t):
            cols = pl.ds(pl.multiple_of(piece * 512 + t * 256, 256), 256)
            out = lax.dot_general(kv[...].reshape(512, 2 * INNER), w[cols, :], nt,
                                  preferred_element_type=F32).reshape(4, LEN, 256)
            for u in (0, 1):
                ek[u, :, cols] = jnp.where(c == 0, out[2 * u], out[2 * u + 1])
                es[u, :, cols] = jnp.where(c == 0, out[2 * u + 1], out[2 * u]).astype(BF)

        cols = pl.ds(piece * 512, 512)
        send(es.at[:, :, cols], er.at[:, :, cols], E1 + piece, core)

    def enc_pair(piece):
        cols = pl.ds(piece * 512, 512)
        got(er.at[:, :, cols], E1 + piece)
        ys[:, cols] = (ek[1 - yh, :, cols] + er[1 - yh, :, cols].astype(F32)).astype(BF)
        send(ys.at[:, cols], yr.at[:, cols], E2 + piece, partner)
        ek[yh, :, cols] = ek[yh, :, cols] + er[yh, :, cols].astype(F32)

    def enc_last(piece):
        cols = pl.ds(piece * 512, 512)
        got(yr.at[:, cols], E2 + piece)
        ek[yh, :, cols] = ek[yh, :, cols] + yr[:, cols].astype(F32)

    attend(0, 0)
    attend(1, 1)
    got(encb.at[4 + p], ENC + 2)
    send(encb.at[4 + p], encb.at[4 + p], ENC + 5, core)
    transpose(4 + p)
    got(encb.at[4 + pp], ENC + 3)
    send(encb.at[4 + pp], encb.at[4 + pp], ENC + 6, core)
    transpose(4 + pp)
    got(encb.at[4 + po], ENC + 5)
    transpose(4 + po)
    got(encb.at[4 + ppo], ENC + 6)
    transpose(4 + ppo)
    weight(0, 0)
    send1(0)
    attend(2, 0)
    weight(1, 1)
    send1(1)
    attend(3, 1)
    out_q = pltpu.make_async_copy(gqb, gq_hbm.at[0], lsem.at[3])
    out_q.start()
    weight(2, 0)
    send1(2)
    weight(3, 1)
    send1(3)
    enc_term(0)
    enc_term(1)
    reduce1(0)
    enc_term(2)
    enc_pair(0)
    enc_term(3)
    enc_pair(1)
    reduce1(1)
    enc_pair(2)
    enc_pair(3)
    reduce2(0)
    reduce1(2)
    reduce2(1)
    for piece in range(4):
        enc_last(piece)
    out_e = pltpu.make_async_copy(ek.at[yh], genc_hbm.at[0], lsem.at[4])
    out_e.start()
    finish(0)
    reduce1(3)
    reduce2(2)
    finish(1)
    reduce2(3)
    finish(2)
    finish(3)
    out_w = pltpu.make_async_copy(outb, gkv_hbm.at[0], lsem.at[5])
    out_w.start()
    for cp in sends:
        cp.wait_send()
    out_q.wait()
    out_e.wait()
    out_w.wait()


def per_device(enc_out, kv_weight, queries, out_grad):
    anywhere = pl.BlockSpec(memory_space=pl.ANY)
    vm = pltpu.VMEM
    return pl.pallas_call(
        body,
        out_shape=(
            jax.ShapeDtypeStruct((1, 64, 2 * INNER), F32),
            jax.ShapeDtypeStruct((1, LEN, D), F32),
            jax.ShapeDtypeStruct((1, 4, Q, INNER), BF),
        ),
        in_specs=[anywhere] * 4,
        out_specs=(anywhere,) * 3,
        scratch_shapes=[
            vm((D, 2 * INNER), BF),
            vm((8, LEN, D), BF),
            vm((D, 8 * LEN), BF),
            vm((4, LEN, 2 * INNER), BF),
            vm((4, Q, INNER), BF),
            vm((4, Q, INNER), BF),
            vm((4, 2, 4, Q, HD), BF),
            vm((4, Q, INNER), BF),
            vm((4, 2, 4, Q, LEN), BF),
            vm((4, 2, 4, Q, LEN), BF),
            vm((2, 8 * LEN, 2 * HD), BF),
            vm((4, 2, 4, 512, HD), BF),
            vm((4, 2, 3, 512, HD), BF),
            vm((4, 2, 3, 128, HD), BF),
            vm((4, 2, 64, HD), BF),
            vm((4, 2, 64, HD), BF),
            vm((64, 2 * INNER), F32),
            vm((2, LEN, D), F32),
            vm((2, LEN, D), BF),
            vm((2, LEN, D), BF),
            vm((LEN, D), BF),
            vm((LEN, D), BF),
            pltpu.SemaphoreType.DMA((6,)),
            pltpu.SemaphoreType.DMA((16,)),
            pltpu.SemaphoreType.DMA((NSEM,)),
            pltpu.SemaphoreType.DMA((NSEM,)),
        ],
        compiler_params=pltpu.CompilerParams(
            collective_id=0, has_side_effects=True, vmem_limit_bytes=62 * 1024 * 1024),
        name="kv_backward",
    )(enc_out, kv_weight, queries, out_grad)


def solution(mesh):
    placed = (
        P("pipe", "dp", None),
        P("pipe", None, None),
        P("pipe", None, "dp", None),
        P("pipe", None, "dp", None),
    )
    return jax.shard_map(
        per_device,
        mesh=mesh,
        in_specs=placed,
        out_specs=(P("pipe", "dp", None), P("pipe", "dp", None), P("pipe", None, "dp", None)),
        check_vma=False,
    )
```

time: 544 us -> 120 us (0.22)
  waiting for transfers between devices: 421 us -> 0 us
  Pallas kernels: 0 us -> 112 us
  matrix products: 52.5 us -> 0 us
  local copies, waits for them, and re-layouts: 48.5 us -> 6.44 us
  between operations: 13.8 us -> 0.64 us
  other arithmetic: 5.77 us -> 0 us
    unnamed x4 -> x0, waiting for transfers between devices: 346 us -> none
    pallas_call x0 -> x1, Pallas kernels: none -> 112 us  [per_device(): pl.pallas_call(body, out_shape=(jax.ShapeDtypeStruct((1, 64, 2 * INNER),...]
    dot_general x8 -> x0, matrix products: 52.5 us -> none  [the longest x1 16.6 us: per_device(): jnp.einsum('mtd,mtc->dc', gathered, kv_grad, preferred_element_type=jnp.f...]
    reduce_scatter x1 -> x0, waiting for transfers between devices: 47.8 us -> none  [per_device(): lax.psum_scatter(enc_term, 'pipe', scatter_dimension=0, tiled=True)]
    unnamed x13 -> x3, local copies, waits for them, and re-layouts: 40.5 us -> 6.44 us
    all_gather x1 -> x0, waiting for transfers between devices: 27.8 us -> none  [per_device(): gathered = lax.all_gather(enc_out, 'pipe', axis=0, tiled=True)]
  transfers between devices with their start and end apart: 3 -> 0, of which waited for: 3 -> 0; matrix products, arithmetic and copies ran while one was open for 4% -> 0% of each run, Pallas kernels for 0% -> 0%
where the time goes in v1:
time: 120 us; the launch traced here: 119 us
  Pallas kernels  112 us (93%)
  local copies, waits for them, and re-layouts  6.44 us (5%)
    pallas_call x1, Pallas kernels, per_device(): pl.pallas_call(body, out_shape=(jax.ShapeDtypeStruct((1, 64, 2 * INNER),...  112 us
    unnamed x3, local copies, waits for them, and re-layouts  6.44 us

profile of v1, /device:TPU:0, one launch (start us, length us, event | category | flops | bytes accessed | tf_op | source)
XLA Modules:
  0.0 119.4 jit_solution(6589588942959396468)
XLA Ops:
  0.6 112.3 %kv_backward.1 = (f32[1,64,4096]{2,1,0:T(8,128)}, f32[1,128,2048]{2,1,0:T(8,128)}, bf16[1,4,32,2048]{3,2,1,0:T(8,128)(2,1)}) custom-call(bf16[1,128,2048]{2,1,0:T(8,128)(2,1)} %enc_hbm.1, bf16[1,2048,4096]{2,1,0:T(8,128)(2,1)} %w_hbm.1, bf16[1,4,32,2048]{3,2,1,0:T(8,128)(2,1)} %q_hbm.1, bf16[1,4,32,2048]{3,2,1,0:T(8,128)(2,1)} %g_hbm.1), custom_call_target="tpu_custom_call" | custom-call | tf_op jit(solution)/shard_map/kv_backward/pallas_call | solution.py:320
  112.9 2.3 %copy.10 = f32[1,64,4096]{2,1,0:T(8,128)} copy(f32[1,64,4096]{2,1,0:T(8,128)} %get-tuple-element.6) | data formatting | bytes 2097152
  115.2 2.3 %copy.11 = f32[1,128,2048]{2,1,0:T(8,128)} copy(f32[1,128,2048]{2,1,0:T(8,128)} %get-tuple-element.7) | data formatting | bytes 2097152
  117.5 1.9 %copy.12 = bf16[1,4,32,2048]{3,2,1,0:T(8,128)(2,1)} copy(bf16[1,4,32,2048]{3,2,1,0:T(8,128)(2,1)} %get-tuple-element.8) | data formatting | bytes 1048576

commit v2 on v1

--- a/solution.py
+++ b/solution.py
@@ -14,11 +14,11 @@
 F32 = jnp.float32
 MESH = pl.DeviceIdType.MESH
 
-ENC, QG, SC, P1, P2, P3, E1, E2, NSEM = 0, 7, 15, 19, 43, 67, 75, 79, 83
+ENC, QG, SC, P1, P2, P3, E1, E2, NSEM = 0, 10, 18, 22, 70, 94, 102, 106, 110
 
 
 def body(enc_hbm, w_hbm, q_hbm, g_hbm, gkv_hbm, genc_hbm, gq_hbm,
-         w, encb, enct, kv, qb, gb, qgn, gqb, sco, sci, rhs, part, r1, r2, x3, r3, outb,
+         w, encb, enct, kv, qb, gb, qgn, gqb, sco, sci, rhs, part, f1, r1, r2, x3, outb,
          ek, es, er, ys, yr, lsem, wsem, ssem, rsem):
     p = lax.axis_index("pipe")
     d = lax.axis_index("dp")
@@ -72,8 +72,12 @@
         cp.start()
         sends.append(cp)
 
+    top, low_rows = pl.ds(0, 64), pl.ds(64, 64)
     send(enc_hbm.at[0], encb.at[p], ENC + 0, core)
-    send(enc_hbm.at[0], encb.at[p], ENC + 1, partner)
+    send(enc_hbm.at[0, top], encb.at[4 + p, top], ENC + 1, near)
+    send(enc_hbm.at[0, low_rows], encb.at[4 + p, low_rows], ENC + 3, far)
+    send(enc_hbm.at[0, low_rows], encb.at[4 + p, low_rows], ENC + 2, near)
+    send(enc_hbm.at[0, top], encb.at[4 + p, top], ENC + 4, far)
 
     def project(first, j):
         cols = pl.ds(pl.multiple_of(j * 256, 256), 256)
@@ -92,25 +96,41 @@
     own_enc.wait()
     got(encb.at[po], ENC + 0)
 
-    @pl.loop(0, 16)
-    def _(j):
-        w_copy(j).wait()
-        project(2 * yh, j)
-
+    def local_kv(lo, hi):
+        @pl.loop(lo, hi)
+        def _(j):
+            w_copy(j).wait()
+            project(2 * yh, j)
+
+    local_kv(0, 8)
+    transpose(p)
+    transpose(po)
+    got(encb.at[4 + p, top], ENC + 1)
+    send(encb.at[4 + p, top], encb.at[p, top], ENC + 5, far)
+    got(encb.at[4 + pp, low_rows], ENC + 3)
+    send(encb.at[4 + pp, low_rows], encb.at[pp, low_rows], ENC + 6, near)
     own_q.wait()
     own_g.wait()
-    send(enc_hbm.at[0], encb.at[4 + p], ENC + 2, near)
-    send(enc_hbm.at[0], encb.at[4 + p], ENC + 3, far)
     for i in range(4):
         cols = pl.ds(pl.multiple_of((1 - yl) * 1024 + i * 256, 256), 256)
         send(qb.at[:, :, cols], qgn.at[i, 0], QG + 2 * i, near)
         send(gb.at[:, :, cols], qgn.at[i, 1], QG + 2 * i + 1, near)
-    transpose(p)
-    transpose(po)
-    got(encb.at[pp], ENC + 1)
-    send(encb.at[pp], encb.at[pp], ENC + 4, core)
+    local_kv(8, 16)
+    got(encb.at[4 + p, low_rows], ENC + 2)
+    send(encb.at[4 + p], encb.at[4 + p], ENC + 7, core)
+    got(encb.at[4 + pp, top], ENC + 4)
+    send(encb.at[4 + pp], encb.at[4 + pp], ENC + 8, core)
+    transpose(4 + p)
+    transpose(4 + pp)
+    got(encb.at[pp, top], ENC + 5)
+    got(encb.at[pp, low_rows], ENC + 6)
+    send(encb.at[pp], encb.at[pp], ENC + 9, core)
     transpose(pp)
-    got(encb.at[ppo], ENC + 4)
+    got(encb.at[4 + po], ENC + 7)
+    transpose(4 + po)
+    got(encb.at[4 + ppo], ENC + 8)
+    transpose(4 + ppo)
+    got(encb.at[ppo], ENC + 9)
     transpose(ppo)
 
     tl = (((0,), (0,)), ((), ()))
@@ -182,23 +202,47 @@
     first = (x, z)
     second = (z, x)
 
-    def send1(i):
+    hi_rows, lo_rows = pl.ds(0, 256), pl.ds(256, 256)
+
+    def alpha(i):
         for half in (0, 1):
-            for k in (1, 2, 3):
-                send(part.at[i, half, lax.rem(first[half] + k, 4)], r1.at[i, half, k - 1],
-                     P1 + (2 * i + half) * 3 + k - 1, peer(half, k))
+            a, sem = first[half], P1 + (2 * i + half) * 6
+            up, down, across = lax.rem(a + 1, 4), lax.rem(a + 3, 4), lax.rem(a + 2, 4)
+            send(part.at[i, half, across, hi_rows], f1.at[i, half, 0], sem, peer(half, 1))
+            send(part.at[i, half, across, lo_rows], f1.at[i, half, 1], sem + 1, peer(half, 3))
+            send(part.at[i, half, up, lo_rows], r1.at[i, half, 0, lo_rows], sem + 2, peer(half, 1))
+            send(part.at[i, half, down, hi_rows], r1.at[i, half, 1, hi_rows], sem + 3, peer(half, 3))
+
+    def beta(i):
+        for half in (0, 1):
+            a, sem = first[half], P1 + (2 * i + half) * 6
+            for way, rows, k in ((0, hi_rows, 1), (1, lo_rows, 3)):
+                got(f1.at[i, half, way], sem + way)
+                block = lax.rem(a + k, 4)
+
+                @pl.loop(0, 4)
+                def _(b):
+                    src = pl.ds(pl.multiple_of(b * 64, 64), 64)
+                    dst = pl.ds(pl.multiple_of(way * 256 + b * 64, 64), 64)
+                    acc = part[i, half, block, dst].astype(F32) + f1[i, half, way, src].astype(F32)
+                    part[i, half, block, dst] = acc.astype(BF)
+
+                send(part.at[i, half, block, rows], r1.at[i, half, way, rows], sem + 4 + way,
+                     peer(half, k))
 
     def reduce1(i):
         for half in (0, 1):
-            a = first[half]
-            for k in (1, 2, 3):
-                got(r1.at[i, half, k - 1], P1 + (2 * i + half) * 3 + k - 1)
+            a, sem = first[half], P1 + (2 * i + half) * 6
+            got(r1.at[i, half, 0, lo_rows], sem + 2)
+            got(r1.at[i, half, 1, hi_rows], sem + 3)
+            got(r1.at[i, half, 0, hi_rows], sem + 4)
+            got(r1.at[i, half, 1, lo_rows], sem + 5)
 
             @pl.loop(0, 8)
             def _(b):
                 rows = pl.ds(pl.multiple_of(b * 64, 64), 64)
                 acc = part[i, half, a, rows].astype(F32)
-                for k in range(3):
+                for k in range(2):
                     acc += r1[i, half, k, rows].astype(F32)
                 part[i, half, a, rows] = acc.astype(BF)
 
@@ -222,15 +266,14 @@
                 return acc
 
             x3[i, half] = total(1 - yl).astype(BF)
-            send(x3.at[i, half], r3.at[i, half], P3 + 2 * i + half, near)
             cols = pl.ds(pl.multiple_of(half * INNER + (yl * 4 + i) * HD, HD), HD)
-            outb[:, cols] = total(yl)
+            send(x3.at[i, half], outb.at[:, cols], P3 + 2 * i + half, near)
+            outb[:, cols] = total(yl).astype(BF)
 
     def finish(i):
         for half in (0, 1):
-            got(r3.at[i, half], P3 + 2 * i + half)
             cols = pl.ds(pl.multiple_of(half * INNER + ((1 - yl) * 4 + i) * HD, HD), HD)
-            outb[:, cols] = r3[i, half].astype(F32)
+            got(outb.at[:, cols], P3 + 2 * i + half)
 
     def enc_term(piece):
         @pl.loop(0, 2)
@@ -259,52 +302,44 @@
 
     attend(0, 0)
     attend(1, 1)
-    got(encb.at[4 + p], ENC + 2)
-    send(encb.at[4 + p], encb.at[4 + p], ENC + 5, core)
-    transpose(4 + p)
-    got(encb.at[4 + pp], ENC + 3)
-    send(encb.at[4 + pp], encb.at[4 + pp], ENC + 6, core)
-    transpose(4 + pp)
-    got(encb.at[4 + po], ENC + 5)
-    transpose(4 + po)
-    got(encb.at[4 + ppo], ENC + 6)
-    transpose(4 + ppo)
     weight(0, 0)
-    send1(0)
+    alpha(0)
     attend(2, 0)
     weight(1, 1)
-    send1(1)
+    alpha(1)
+    beta(0)
     attend(3, 1)
     out_q = pltpu.make_async_copy(gqb, gq_hbm.at[0], lsem.at[3])
     out_q.start()
     weight(2, 0)
-    send1(2)
+    alpha(2)
+    beta(1)
     weight(3, 1)
-    send1(3)
+    alpha(3)
     enc_term(0)
+    reduce1(0)
+    beta(2)
     enc_term(1)
-    reduce1(0)
+    beta(3)
+    enc_pair(0)
     enc_term(2)
-    enc_pair(0)
+    reduce1(1)
+    enc_pair(1)
     enc_term(3)
-    enc_pair(1)
-    reduce1(1)
     enc_pair(2)
+    reduce2(0)
     enc_pair(3)
-    reduce2(0)
     reduce1(2)
     reduce2(1)
     for piece in range(4):
         enc_last(piece)
     out_e = pltpu.make_async_copy(ek.at[yh], genc_hbm.at[0], lsem.at[4])
     out_e.start()
-    finish(0)
     reduce1(3)
     reduce2(2)
-    finish(1)
     reduce2(3)
-    finish(2)
-    finish(3)
+    for i in range(4):
+        finish(i)
     out_w = pltpu.make_async_copy(outb, gkv_hbm.at[0], lsem.at[5])
     out_w.start()
     for cp in sends:
@@ -314,13 +349,32 @@
     out_w.wait()
 
 
+def hand_over(gkv, genc, gq, gkv_out, genc_out, gq_out, low, wide, enc, query, isem, osem):
+    loads = [pltpu.make_async_copy(src.at[0], dst, isem.at[n])
+             for n, (src, dst) in enumerate(((gkv, low), (genc, enc), (gq, query)))]
+    stores = [pltpu.make_async_copy(src, dst.at[0], osem.at[n])
+              for n, (src, dst) in enumerate(((wide, gkv_out), (enc, genc_out), (query, gq_out)))]
+    for cp in loads:
+        cp.start()
+    for n, (load, store) in enumerate(zip(loads, stores)):
+        load.wait()
+        if n == 0:
+            @pl.loop(0, 8)
+            def _(b):
+                cols = pl.ds(pl.multiple_of(b * 512, 512), 512)
+                wide[:, cols] = low[:, cols].astype(F32)
+        store.start()
+    for cp in stores:
+        cp.wait()
+
+
 def per_device(enc_out, kv_weight, queries, out_grad):
     anywhere = pl.BlockSpec(memory_space=pl.ANY)
     vm = pltpu.VMEM
-    return pl.pallas_call(
+    gkv, genc, gq = pl.pallas_call(
         body,
         out_shape=(
-            jax.ShapeDtypeStruct((1, 64, 2 * INNER), F32),
+            jax.ShapeDtypeStruct((1, 64, 2 * INNER), BF),
             jax.ShapeDtypeStruct((1, LEN, D), F32),
             jax.ShapeDtypeStruct((1, 4, Q, INNER), BF),
         ),
@@ -339,11 +393,11 @@
             vm((4, 2, 4, Q, LEN), BF),
             vm((2, 8 * LEN, 2 * HD), BF),
             vm((4, 2, 4, 512, HD), BF),
-            vm((4, 2, 3, 512, HD), BF),
+            vm((4, 2, 2, 256, HD), BF),
+            vm((4, 2, 2, 512, HD), BF),
             vm((4, 2, 3, 128, HD), BF),
             vm((4, 2, 64, HD), BF),
-            vm((4, 2, 64, HD), BF),
-            vm((64, 2 * INNER), F32),
+            vm((64, 2 * INNER), BF),
             vm((2, LEN, D), F32),
             vm((2, LEN, D), BF),
             vm((2, LEN, D), BF),
@@ -358,6 +412,26 @@
             collective_id=0, has_side_effects=True, vmem_limit_bytes=62 * 1024 * 1024),
         name="kv_backward",
     )(enc_out, kv_weight, queries, out_grad)
+    return pl.pallas_call(
+        hand_over,
+        out_shape=(
+            jax.ShapeDtypeStruct((1, 64, 2 * INNER), F32),
+            jax.ShapeDtypeStruct((1, LEN, D), F32),
+            jax.ShapeDtypeStruct((1, 4, Q, INNER), BF),
+        ),
+        in_specs=[anywhere] * 3,
+        out_specs=(anywhere,) * 3,
+        scratch_shapes=[
+            vm((64, 2 * INNER), BF),
+            vm((64, 2 * INNER), F32),
+            vm((LEN, D), F32),
+            vm((4, Q, INNER), BF),
+            pltpu.SemaphoreType.DMA((3,)),
+            pltpu.SemaphoreType.DMA((3,)),
+        ],
+        compiler_params=pltpu.CompilerParams(vmem_limit_bytes=16 * 1024 * 1024),
+        name="hand_over",
+    )(gkv, genc, gq)
 
 
 def solution(mesh):

time: 120 us -> 103 us (0.86)
  Pallas kernels: 112 us -> 98.3 us
  local copies, waits for them, and re-layouts: 6.44 us -> 3.3 us
    pallas_call x1, Pallas kernels: 112 us -> 96.6 us  [per_device(): pl.pallas_call(body, out_shape=(jax.ShapeDtypeStruct((1, 64, 2 * INNER),...]
    unnamed x3 -> x6, local copies, waits for them, and re-layouts: 6.44 us -> 3.3 us
    pallas_call x0 -> x1, Pallas kernels: none -> 1.77 us  [per_device(): pl.pallas_call(hand_over, out_shape=(jax.ShapeDtypeStruct((1, 64, 2 * INN...]
where the time goes in v2:
time: 103 us; the launch traced here: 102 us
  Pallas kernels  98.3 us (95%)
  local copies, waits for them, and re-layouts  3.3 us (3%)
    pallas_call x1, Pallas kernels, per_device(): pl.pallas_call(body, out_shape=(jax.ShapeDtypeStruct((1, 64, 2 * INNER),...  96.6 us
    unnamed x6, local copies, waits for them, and re-layouts  3.3 us

profile of v2, /device:TPU:0, one launch (start us, length us, event | category | flops | bytes accessed | tf_op | source)
XLA Modules:
  0.0 102.4 jit_solution(8725270654167163831)
XLA Ops:
  0.6 96.6 %kv_backward.1 = (bf16[1,64,4096]{2,1,0:T(8,128)(2,1)}, f32[1,128,2048]{2,1,0:T(8,128)}, bf16[1,4,32,2048]{3,2,1,0:T(8,128)(2,1)}) custom-call(bf16[1,128,2048]{2,1,0:T(8,128)(2,1)} %enc_hbm.1, bf16[1,2048,4096]{2,1,0:T(8,128)(2,1)} %w_hbm.1, bf16[1,4,32,2048]{3,2,1,0:T(8,128)(2,1)} %q_hbm.1, bf16[1,4,32,2048]{3,2,1,0:T(8,128)(2,1)} %g_hbm.1), custom_call_target="tpu_custom_call" | custom-call | tf_op jit(solution)/shard_map/kv_backward/pallas_call | solution.py:374
  97.2 0.0 copy-start
  97.2 1.2 %copy-done = f32[1,128,2048]{2,1,0:T(8,128)S(1)} copy-done((f32[1,128,2048]{2,1,0:T(8,128)S(1)}, f32[1,128,2048]{2,1,0:T(8,128)}, u32[]{:S(2)}) %copy-start) | copy-done | bytes 1048600
  98.4 0.0 copy-start.1
  98.4 1.0 %copy-done.1 = bf16[1,64,4096]{2,1,0:T(8,128)(2,1)S(1)} copy-done((bf16[1,64,4096]{2,1,0:T(8,128)(2,1)S(1)}, bf16[1,64,4096]{2,1,0:T(8,128)(2,1)}, u32[]{:S(2)}) %copy-start.1) | copy-done | bytes 524312
  99.5 0.0 copy-start.2
  99.5 1.0 %copy-done.2 = bf16[1,4,32,2048]{3,2,1,0:T(8,128)(2,1)S(1)} copy-done((bf16[1,4,32,2048]{3,2,1,0:T(8,128)(2,1)S(1)}, bf16[1,4,32,2048]{3,2,1,0:T(8,128)(2,1)}, u32[]{:S(2)}) %copy-start.2) | copy-done | bytes 524312
  100.5 1.8 %hand_over.1 = (f32[1,64,4096]{2,1,0:T(8,128)}, f32[1,128,2048]{2,1,0:T(8,128)}, bf16[1,4,32,2048]{3,2,1,0:T(8,128)(2,1)}) custom-call(bf16[1,64,4096]{2,1,0:T(8,128)(2,1)S(1)} %copy-done.1, f32[1,128,2048]{2,1,0:T(8,128)S(1)} %copy-done, bf16[1,4,32,2048]{3,2,1,0:T(8,128)(2,1)S(1)} %copy-done.2), custom_call_target="tpu_custom_call" | custom-call | tf_op jit(solution)/shard_map/hand_over/pallas_call | solution.py:415
Async XLA Ops:
  97.2 1.2 %copy-start = (f32[1,128,2048]{2,1,0:T(8,128)S(1)}, f32[1,128,2048]{2,1,0:T(8,128)}, u32[]{:S(2)}) copy-start(f32[1,128,2048]{2,1,0:T(8,128)} %get-tuple-element.7.genc) | copy-start | bytes 3145732
  98.4 1.0 %copy-start.1 = (bf16[1,64,4096]{2,1,0:T(8,128)(2,1)S(1)}, bf16[1,64,4096]{2,1,0:T(8,128)(2,1)}, u32[]{:S(2)}) copy-start(bf16[1,64,4096]{2,1,0:T(8,128)(2,1)} %get-tuple-element.6.gkv) | copy-start | bytes 1572868
  99.5 1.0 %copy-start.2 = (bf16[1,4,32,2048]{3,2,1,0:T(8,128)(2,1)S(1)}, bf16[1,4,32,2048]{3,2,1,0:T(8,128)(2,1)}, u32[]{:S(2)}) copy-start(bf16[1,4,32,2048]{3,2,1,0:T(8,128)(2,1)} %get-tuple-element.8.gq) | copy-start | bytes 1572868

commit v3 on v2

--- a/solution.py
+++ b/solution.py
@@ -76,8 +76,6 @@
     send(enc_hbm.at[0], encb.at[p], ENC + 0, core)
     send(enc_hbm.at[0, top], encb.at[4 + p, top], ENC + 1, near)
     send(enc_hbm.at[0, low_rows], encb.at[4 + p, low_rows], ENC + 3, far)
-    send(enc_hbm.at[0, low_rows], encb.at[4 + p, low_rows], ENC + 2, near)
-    send(enc_hbm.at[0, top], encb.at[4 + p, top], ENC + 4, far)
 
     def project(first, j):
         cols = pl.ds(pl.multiple_of(j * 256, 256), 256)
@@ -102,45 +100,38 @@
             w_copy(j).wait()
             project(2 * yh, j)
 
-    local_kv(0, 8)
-    transpose(p)
-    transpose(po)
+    def send_factors(i):
+        cols = pl.ds(pl.multiple_of((1 - yl) * 1024 + i * 256, 256), 256)
+        send(qb.at[:, :, cols], qgn.at[i, 0], QG + 2 * i, near)
+        send(gb.at[:, :, cols], qgn.at[i, 1], QG + 2 * i + 1, near)
+
+    local_kv(0, 4)
     got(encb.at[4 + p, top], ENC + 1)
     send(encb.at[4 + p, top], encb.at[p, top], ENC + 5, far)
     got(encb.at[4 + pp, low_rows], ENC + 3)
     send(encb.at[4 + pp, low_rows], encb.at[pp, low_rows], ENC + 6, near)
     own_q.wait()
     own_g.wait()
-    for i in range(4):
-        cols = pl.ds(pl.multiple_of((1 - yl) * 1024 + i * 256, 256), 256)
-        send(qb.at[:, :, cols], qgn.at[i, 0], QG + 2 * i, near)
-        send(gb.at[:, :, cols], qgn.at[i, 1], QG + 2 * i + 1, near)
-    local_kv(8, 16)
-    got(encb.at[4 + p, low_rows], ENC + 2)
-    send(encb.at[4 + p], encb.at[4 + p], ENC + 7, core)
-    got(encb.at[4 + pp, top], ENC + 4)
-    send(encb.at[4 + pp], encb.at[4 + pp], ENC + 8, core)
-    transpose(4 + p)
-    transpose(4 + pp)
+    local_kv(4, 13)
     got(encb.at[pp, top], ENC + 5)
     got(encb.at[pp, low_rows], ENC + 6)
     send(encb.at[pp], encb.at[pp], ENC + 9, core)
-    transpose(pp)
-    got(encb.at[4 + po], ENC + 7)
-    transpose(4 + po)
-    got(encb.at[4 + ppo], ENC + 8)
-    transpose(4 + ppo)
+    send(enc_hbm.at[0, low_rows], encb.at[4 + p, low_rows], ENC + 2, near)
+    send(enc_hbm.at[0, top], encb.at[4 + p, top], ENC + 4, far)
+    send_factors(0)
+    local_kv(13, 16)
+    transpose(p)
     got(encb.at[ppo], ENC + 9)
-    transpose(ppo)
 
     tl = (((0,), (0,)), ((), ()))
     nt = (((1,), (1,)), ((), ()))
 
-    def attend(i, slot):
+    def rest_kv(i):
         @pl.loop(0, 4)
         def _(t):
             project(2 * (1 - yh), i + 4 * t)
 
+    def attend(i, slot):
         units = []
         for own in (0, 1):
             head = (yl if own else 1 - yl) * 4 + i
@@ -184,10 +175,10 @@
             rhs[slot, 512 + m * LEN:512 + (m + 1) * LEN, 0:HD] = kg.astype(BF)
             rhs[slot, 512 + m * LEN:512 + (m + 1) * LEN, HD:2 * HD] = vg.astype(BF)
 
-        @pl.loop(0, 4)
-        def _(xp):
-            rows = pl.ds(pl.multiple_of(xp * 512, 512), 512)
-            for half in (0, 1):
+        for half in (0, 1):
+            @pl.loop(0, 4)
+            def _(xp):
+                rows = pl.ds(pl.multiple_of(xp * 512, 512), 512)
                 out = jnp.dot(enct[rows, :], rhs[slot, :, half * HD:(half + 1) * HD],
                               preferred_element_type=F32).astype(BF)
                 for yy in range(2):
@@ -199,17 +190,23 @@
                             at = pl.multiple_of(xp * 128 + yy * 64, 64)
                             part[i, 1, zz, pl.ds(at, 64)] = piece
 
+            alpha(i, half)
+
     first = (x, z)
     second = (z, x)
 
     hi_rows, lo_rows = pl.ds(0, 256), pl.ds(256, 256)
 
-    def alpha(i):
+    def alpha(i, half):
+        a, sem = first[half], P1 + (2 * i + half) * 6
+        across = lax.rem(a + 2, 4)
+        send(part.at[i, half, across, hi_rows], f1.at[i, half, 0], sem, peer(half, 1))
+        send(part.at[i, half, across, lo_rows], f1.at[i, half, 1], sem + 1, peer(half, 3))
+
+    def direct(i):
         for half in (0, 1):
             a, sem = first[half], P1 + (2 * i + half) * 6
-            up, down, across = lax.rem(a + 1, 4), lax.rem(a + 3, 4), lax.rem(a + 2, 4)
-            send(part.at[i, half, across, hi_rows], f1.at[i, half, 0], sem, peer(half, 1))
-            send(part.at[i, half, across, lo_rows], f1.at[i, half, 1], sem + 1, peer(half, 3))
+            up, down = lax.rem(a + 1, 4), lax.rem(a + 3, 4)
             send(part.at[i, half, up, lo_rows], r1.at[i, half, 0, lo_rows], sem + 2, peer(half, 1))
             send(part.at[i, half, down, hi_rows], r1.at[i, half, 1, hi_rows], sem + 3, peer(half, 3))
 
@@ -300,44 +297,64 @@
         got(yr.at[:, cols], E2 + piece)
         ek[yh, :, cols] = ek[yh, :, cols] + yr[:, cols].astype(F32)
 
+    rest_kv(0)
     attend(0, 0)
+    transpose(po)
+    transpose(pp)
+    transpose(ppo)
+    rest_kv(1)
+    got(encb.at[4 + p, low_rows], ENC + 2)
+    send(encb.at[4 + p], encb.at[4 + p], ENC + 7, core)
+    got(encb.at[4 + pp, top], ENC + 4)
+    send(encb.at[4 + pp], encb.at[4 + pp], ENC + 8, core)
+    send_factors(1)
+    transpose(4 + p)
+    transpose(4 + pp)
+    got(encb.at[4 + po], ENC + 7)
+    transpose(4 + po)
+    got(encb.at[4 + ppo], ENC + 8)
+    transpose(4 + ppo)
+    weight(0, 0)
     attend(1, 1)
-    weight(0, 0)
-    alpha(0)
+    direct(0)
+    send_factors(2)
+    rest_kv(2)
+    beta(0)
+    weight(1, 1)
     attend(2, 0)
-    weight(1, 1)
-    alpha(1)
-    beta(0)
+    direct(1)
+    send_factors(3)
+    rest_kv(3)
+    beta(1)
+    weight(2, 0)
     attend(3, 1)
+    direct(2)
     out_q = pltpu.make_async_copy(gqb, gq_hbm.at[0], lsem.at[3])
     out_q.start()
-    weight(2, 0)
-    alpha(2)
-    beta(1)
-    weight(3, 1)
-    alpha(3)
-    enc_term(0)
     reduce1(0)
     beta(2)
+    weight(3, 1)
+    direct(3)
+    enc_term(0)
+    reduce1(1)
     enc_term(1)
     beta(3)
     enc_pair(0)
+    reduce2(0)
     enc_term(2)
-    reduce1(1)
     enc_pair(1)
+    reduce1(2)
     enc_term(3)
     enc_pair(2)
-    reduce2(0)
+    reduce2(1)
+    reduce1(3)
     enc_pair(3)
-    reduce1(2)
-    reduce2(1)
+    reduce2(2)
+    reduce2(3)
     for piece in range(4):
         enc_last(piece)
     out_e = pltpu.make_async_copy(ek.at[yh], genc_hbm.at[0], lsem.at[4])
     out_e.start()
-    reduce1(3)
-    reduce2(2)
-    reduce2(3)
     for i in range(4):
         finish(i)
     out_w = pltpu.make_async_copy(outb, gkv_hbm.at[0], lsem.at[5])

time: 103 us -> 101 us (0.981)
  Pallas kernels: 98.3 us -> 96.8 us
    pallas_call x1, Pallas kernels: 96.6 us -> 95 us  [per_device(): pl.pallas_call(body, out_shape=(jax.ShapeDtypeStruct((1, 64, 2 * INNER),...]
where the time goes in v3:
time: 101 us
  Pallas kernels  96.8 us (96%)
  local copies, waits for them, and re-layouts  3.3 us (3%)
    pallas_call x1, Pallas kernels, per_device(): pl.pallas_call(body, out_shape=(jax.ShapeDtypeStruct((1, 64, 2 * INNER),...  95 us
    unnamed x6, local copies, waits for them, and re-layouts  3.3 us

profile of v3, /device:TPU:0, one launch (start us, length us, event | category | flops | bytes accessed | tf_op | source)
XLA Modules:
  0.0 100.9 jit_solution(6475753083415251839)
XLA Ops:
  0.6 95.0 %kv_backward.1 = (bf16[1,64,4096]{2,1,0:T(8,128)(2,1)}, f32[1,128,2048]{2,1,0:T(8,128)}, bf16[1,4,32,2048]{3,2,1,0:T(8,128)(2,1)}) custom-call(bf16[1,128,2048]{2,1,0:T(8,128)(2,1)} %enc_hbm.1, bf16[1,2048,4096]{2,1,0:T(8,128)(2,1)} %w_hbm.1, bf16[1,4,32,2048]{3,2,1,0:T(8,128)(2,1)} %q_hbm.1, bf16[1,4,32,2048]{3,2,1,0:T(8,128)(2,1)} %g_hbm.1), custom_call_target="tpu_custom_call" | custom-call | tf_op jit(solution)/shard_map/kv_backward/pallas_call | solution.py:391
  95.6 0.0 copy-start
  95.6 1.2 %copy-done = f32[1,128,2048]{2,1,0:T(8,128)S(1)} copy-done((f32[1,128,2048]{2,1,0:T(8,128)S(1)}, f32[1,128,2048]{2,1,0:T(8,128)}, u32[]{:S(2)}) %copy-start) | copy-done | bytes 1048600
  96.9 0.0 copy-start.1
  96.9 1.0 %copy-done.1 = bf16[1,64,4096]{2,1,0:T(8,128)(2,1)S(1)} copy-done((bf16[1,64,4096]{2,1,0:T(8,128)(2,1)S(1)}, bf16[1,64,4096]{2,1,0:T(8,128)(2,1)}, u32[]{:S(2)}) %copy-start.1) | copy-done | bytes 524312
  97.9 0.0 copy-start.2
  97.9 1.0 %copy-done.2 = bf16[1,4,32,2048]{3,2,1,0:T(8,128)(2,1)S(1)} copy-done((bf16[1,4,32,2048]{3,2,1,0:T(8,128)(2,1)S(1)}, bf16[1,4,32,2048]{3,2,1,0:T(8,128)(2,1)}, u32[]{:S(2)}) %copy-start.2) | copy-done | bytes 524312
  98.9 1.8 %hand_over.1 = (f32[1,64,4096]{2,1,0:T(8,128)}, f32[1,128,2048]{2,1,0:T(8,128)}, bf16[1,4,32,2048]{3,2,1,0:T(8,128)(2,1)}) custom-call(bf16[1,64,4096]{2,1,0:T(8,128)(2,1)S(1)} %copy-done.1, f32[1,128,2048]{2,1,0:T(8,128)S(1)} %copy-done, bf16[1,4,32,2048]{3,2,1,0:T(8,128)(2,1)S(1)} %copy-done.2), custom_call_target="tpu_custom_call" | custom-call | tf_op jit(solution)/shard_map/hand_over/pallas_call | solution.py:432
Async XLA Ops:
  95.6 1.2 %copy-start = (f32[1,128,2048]{2,1,0:T(8,128)S(1)}, f32[1,128,2048]{2,1,0:T(8,128)}, u32[]{:S(2)}) copy-start(f32[1,128,2048]{2,1,0:T(8,128)} %get-tuple-element.7.genc) | copy-start | bytes 3145732
  96.9 1.0 %copy-start.1 = (bf16[1,64,4096]{2,1,0:T(8,128)(2,1)S(1)}, bf16[1,64,4096]{2,1,0:T(8,128)(2,1)}, u32[]{:S(2)}) copy-start(bf16[1,64,4096]{2,1,0:T(8,128)(2,1)} %get-tuple-element.6.gkv) | copy-start | bytes 1572868
  97.9 1.0 %copy-start.2 = (bf16[1,4,32,2048]{3,2,1,0:T(8,128)(2,1)S(1)}, bf16[1,4,32,2048]{3,2,1,0:T(8,128)(2,1)}, u32[]{:S(2)}) copy-start(bf16[1,4,32,2048]{3,2,1,0:T(8,128)(2,1)} %get-tuple-element.8.gq) | copy-start | bytes 1572868

commit v4 on v3

--- a/solution.py
+++ b/solution.py
@@ -332,16 +332,16 @@
     out_q = pltpu.make_async_copy(gqb, gq_hbm.at[0], lsem.at[3])
     out_q.start()
     reduce1(0)
+    weight(3, 1)
     beta(2)
-    weight(3, 1)
     direct(3)
     enc_term(0)
     reduce1(1)
     enc_term(1)
-    beta(3)
     enc_pair(0)
     reduce2(0)
     enc_term(2)
+    beta(3)
     enc_pair(1)
     reduce1(2)
     enc_term(3)

time: 101 us -> 101 us (level)
  no operation moved by 1% of the time
where the time goes in v4:
time: 101 us
  Pallas kernels  96.4 us (95%)
  local copies, waits for them, and re-layouts  3.3 us (3%)
    pallas_call x1, Pallas kernels, per_device(): pl.pallas_call(body, out_shape=(jax.ShapeDtypeStruct((1, 64, 2 * INNER),...  94.6 us
    unnamed x6, local copies, waits for them, and re-layouts  3.3 us

profile of v4, /device:TPU:0, one launch (start us, length us, event | category | flops | bytes accessed | tf_op | source)
XLA Modules:
  0.0 100.5 jit_solution(9313219811447874854)
XLA Ops:
  0.6 94.6 %kv_backward.1 = (bf16[1,64,4096]{2,1,0:T(8,128)(2,1)}, f32[1,128,2048]{2,1,0:T(8,128)}, bf16[1,4,32,2048]{3,2,1,0:T(8,128)(2,1)}) custom-call(bf16[1,128,2048]{2,1,0:T(8,128)(2,1)} %enc_hbm.1, bf16[1,2048,4096]{2,1,0:T(8,128)(2,1)} %w_hbm.1, bf16[1,4,32,2048]{3,2,1,0:T(8,128)(2,1)} %q_hbm.1, bf16[1,4,32,2048]{3,2,1,0:T(8,128)(2,1)} %g_hbm.1), custom_call_target="tpu_custom_call" | custom-call | tf_op jit(solution)/shard_map/kv_backward/pallas_call | solution.py:391
  95.3 0.0 copy-start
  95.3 1.2 %copy-done = f32[1,128,2048]{2,1,0:T(8,128)S(1)} copy-done((f32[1,128,2048]{2,1,0:T(8,128)S(1)}, f32[1,128,2048]{2,1,0:T(8,128)}, u32[]{:S(2)}) %copy-start) | copy-done | bytes 1048600
  96.5 0.0 copy-start.1
  96.5 1.0 %copy-done.1 = bf16[1,64,4096]{2,1,0:T(8,128)(2,1)S(1)} copy-done((bf16[1,64,4096]{2,1,0:T(8,128)(2,1)S(1)}, bf16[1,64,4096]{2,1,0:T(8,128)(2,1)}, u32[]{:S(2)}) %copy-start.1) | copy-done | bytes 524312
  97.5 0.0 copy-start.2
  97.5 1.0 %copy-done.2 = bf16[1,4,32,2048]{3,2,1,0:T(8,128)(2,1)S(1)} copy-done((bf16[1,4,32,2048]{3,2,1,0:T(8,128)(2,1)S(1)}, bf16[1,4,32,2048]{3,2,1,0:T(8,128)(2,1)}, u32[]{:S(2)}) %copy-start.2) | copy-done | bytes 524312
  98.6 1.8 %hand_over.1 = (f32[1,64,4096]{2,1,0:T(8,128)}, f32[1,128,2048]{2,1,0:T(8,128)}, bf16[1,4,32,2048]{3,2,1,0:T(8,128)(2,1)}) custom-call(bf16[1,64,4096]{2,1,0:T(8,128)(2,1)S(1)} %copy-done.1, f32[1,128,2048]{2,1,0:T(8,128)S(1)} %copy-done, bf16[1,4,32,2048]{3,2,1,0:T(8,128)(2,1)S(1)} %copy-done.2), custom_call_target="tpu_custom_call" | custom-call | tf_op jit(solution)/shard_map/hand_over/pallas_call | solution.py:432
Async XLA Ops:
  95.3 1.2 %copy-start = (f32[1,128,2048]{2,1,0:T(8,128)S(1)}, f32[1,128,2048]{2,1,0:T(8,128)}, u32[]{:S(2)}) copy-start(f32[1,128,2048]{2,1,0:T(8,128)} %get-tuple-element.7.genc) | copy-start | bytes 3145732
  96.5 1.0 %copy-start.1 = (bf16[1,64,4096]{2,1,0:T(8,128)(2,1)S(1)}, bf16[1,64,4096]{2,1,0:T(8,128)(2,1)}, u32[]{:S(2)}) copy-start(bf16[1,64,4096]{2,1,0:T(8,128)(2,1)} %get-tuple-element.6.gkv) | copy-start | bytes 1572868
  97.5 1.0 %copy-start.2 = (bf16[1,4,32,2048]{3,2,1,0:T(8,128)(2,1)S(1)}, bf16[1,4,32,2048]{3,2,1,0:T(8,128)(2,1)}, u32[]{:S(2)}) copy-start(bf16[1,4,32,2048]{3,2,1,0:T(8,128)(2,1)} %get-tuple-element.8.gq) | copy-start | bytes 1572868

commit v5 on v4

--- a/solution.py
+++ b/solution.py
@@ -347,8 +347,8 @@
     enc_term(3)
     enc_pair(2)
     reduce2(1)
+    enc_pair(3)
     reduce1(3)
-    enc_pair(3)
     reduce2(2)
     reduce2(3)
     for piece in range(4):

time: 101 us -> 100 us (0.990)
  no operation moved by 1% of the time
where the time goes in v5:
time: 100 us; the launch traced here: 99.8 us
  Pallas kernels  95.7 us (96%)
  local copies, waits for them, and re-layouts  3.3 us (3%)
    pallas_call x1, Pallas kernels, per_device(): pl.pallas_call(body, out_shape=(jax.ShapeDtypeStruct((1, 64, 2 * INNER),...  93.9 us
    unnamed x6, local copies, waits for them, and re-layouts  3.3 us

profile of v5, /device:TPU:0, one launch (start us, length us, event | category | flops | bytes accessed | tf_op | source)
XLA Modules:
  0.0 99.8 jit_solution(2564910344691931609)
XLA Ops:
  0.6 93.9 %kv_backward.1 = (bf16[1,64,4096]{2,1,0:T(8,128)(2,1)}, f32[1,128,2048]{2,1,0:T(8,128)}, bf16[1,4,32,2048]{3,2,1,0:T(8,128)(2,1)}) custom-call(bf16[1,128,2048]{2,1,0:T(8,128)(2,1)} %enc_hbm.1, bf16[1,2048,4096]{2,1,0:T(8,128)(2,1)} %w_hbm.1, bf16[1,4,32,2048]{3,2,1,0:T(8,128)(2,1)} %q_hbm.1, bf16[1,4,32,2048]{3,2,1,0:T(8,128)(2,1)} %g_hbm.1), custom_call_target="tpu_custom_call" | custom-call | tf_op jit(solution)/shard_map/kv_backward/pallas_call | solution.py:391
  94.5 0.0 copy-start
  94.6 1.2 %copy-done = f32[1,128,2048]{2,1,0:T(8,128)S(1)} copy-done((f32[1,128,2048]{2,1,0:T(8,128)S(1)}, f32[1,128,2048]{2,1,0:T(8,128)}, u32[]{:S(2)}) %copy-start) | copy-done | bytes 1048600
  95.8 0.0 copy-start.1
  95.8 1.0 %copy-done.1 = bf16[1,64,4096]{2,1,0:T(8,128)(2,1)S(1)} copy-done((bf16[1,64,4096]{2,1,0:T(8,128)(2,1)S(1)}, bf16[1,64,4096]{2,1,0:T(8,128)(2,1)}, u32[]{:S(2)}) %copy-start.1) | copy-done | bytes 524312
  96.8 0.0 copy-start.2
  96.8 1.0 %copy-done.2 = bf16[1,4,32,2048]{3,2,1,0:T(8,128)(2,1)S(1)} copy-done((bf16[1,4,32,2048]{3,2,1,0:T(8,128)(2,1)S(1)}, bf16[1,4,32,2048]{3,2,1,0:T(8,128)(2,1)}, u32[]{:S(2)}) %copy-start.2) | copy-done | bytes 524312
  97.9 1.8 %hand_over.1 = (f32[1,64,4096]{2,1,0:T(8,128)}, f32[1,128,2048]{2,1,0:T(8,128)}, bf16[1,4,32,2048]{3,2,1,0:T(8,128)(2,1)}) custom-call(bf16[1,64,4096]{2,1,0:T(8,128)(2,1)S(1)} %copy-done.1, f32[1,128,2048]{2,1,0:T(8,128)S(1)} %copy-done, bf16[1,4,32,2048]{3,2,1,0:T(8,128)(2,1)S(1)} %copy-done.2), custom_call_target="tpu_custom_call" | custom-call | tf_op jit(solution)/shard_map/hand_over/pallas_call | solution.py:432
Async XLA Ops:
  94.5 1.2 %copy-start = (f32[1,128,2048]{2,1,0:T(8,128)S(1)}, f32[1,128,2048]{2,1,0:T(8,128)}, u32[]{:S(2)}) copy-start(f32[1,128,2048]{2,1,0:T(8,128)} %get-tuple-element.7.genc) | copy-start | bytes 3145732
  95.8 1.0 %copy-start.1 = (bf16[1,64,4096]{2,1,0:T(8,128)(2,1)S(1)}, bf16[1,64,4096]{2,1,0:T(8,128)(2,1)}, u32[]{:S(2)}) copy-start(bf16[1,64,4096]{2,1,0:T(8,128)(2,1)} %get-tuple-element.6.gkv) | copy-start | bytes 1572868
  96.8 1.0 %copy-start.2 = (bf16[1,4,32,2048]{3,2,1,0:T(8,128)(2,1)S(1)}, bf16[1,4,32,2048]{3,2,1,0:T(8,128)(2,1)}, u32[]{:S(2)}) copy-start(bf16[1,4,32,2048]{3,2,1,0:T(8,128)(2,1)} %get-tuple-element.8.gq) | copy-start | bytes 1572868
